TPU v7x, 32 devices: a whole 2x2x4 slice. The times are simulated.
32 devices in a mesh: seq: 16 (over z, y, x), head: 2 (over core).
Axes of the slice: x: 2, y: 2, z: 4, core: 2. Of those that a mesh axis runs over, the one named last changes fastest.
Arguments:
- hidden: bfloat16 [2048, 2048], P('seq'), may hold values from -6 to 6
- queries: bfloat16 [2048, 3072], P('seq', 'head'), may hold values from -90 to 90
- req_len: int32 [2], replicated, may hold values from 1 to 1920, 2048 in all
- req_offset: int32 [2], replicated, may hold values from 0 to 4095
- expert_ids: int32 [2048, 6], P('seq'), may hold values from 0 to 15, all different within a row; in each aligned block of 128 rows (0 to 127, 128 to 255, ...) at most 64 rows name the same one
- decode_slot: int32 [128], replicated, may hold values from 0 to 127, as said below
- attn_gain: float32 [2048], replicated, may hold values from 0.25 to 1.75
- kv_down: bfloat16 [2048, 576], replicated, may hold values from -0.125 to 0.125
- kv_gain: float32 [512], replicated, may hold values from 0.25 to 1.75
- key_up: bfloat16 [16, 128, 512], P('head'), may hold values from -0.5 to 0.5
- value_up: bfloat16 [16, 512, 128], P('head'), may hold values from -0.25 to 0.25
- out_proj: bfloat16 [2048, 2048], P('head'), may hold values from -0.5 to 0.5
- ffn_gain: float32 [2048], replicated, may hold values from 0.25 to 1.75
- router: float32 [2048, 16], replicated, may hold values from -0.125 to 0.125
- expert_gate_up: bfloat16 [16, 2, 2048, 1408], P('seq', None, None, 'head'), may hold values from -0.125 to 0.125
- expert_down: bfloat16 [16, 1408, 2048], P('seq', 'head'), may hold values from -0.15625 to 0.15625
Outputs:
- output: bfloat16 [2048, 2048], P('seq', 'head')
- decode_latent: bfloat16 [128, 16, 512], P(('seq', 'head'))
- decode_rope: bfloat16 [128, 1024], P(('seq', 'head'))
Inputs may be any that keep to these rules, and one draw needn't show every extreme that they name: `req_len`: the lengths sum to 2048. `expert_ids`: the 128 rows of one index of seq name one expert at most 64 times in all. `decode_slot`: all entries differ; slot g belongs to device g // 4 in the order seq then head, and all 4 slots of some device are named.
All inputs are finite; a program needn't handle non-finite values.
Results may differ from a plain program's by a relative error of at most 0.02.
Values may be sent and summed in bfloat16 or wider, within the bound.
A program may use at most 128 MiB of HBM per device.

v0:
```python
import math
import jax
import jax.numpy as jnp
from jax import lax
from jax.sharding import PartitionSpec as P

D = 2048
NOPE = 128
ROPE = 64
V_HEAD = 128
KV_RANK = 512
TOP = 6
BLOCK = 16
DEC_SLOTS = 4
ROPE_BASE = 50000.0
ROUTE_SCALE = 2.446
EPSILON = 1e-06
MASKED = -1e30


def rms_rows(values, scale_gain):
    values = values.astype(jnp.float32)
    inverse = lax.rsqrt(jnp.mean(values * values, axis=-1, keepdims=True) + EPSILON)
    return values * inverse * scale_gain


def angles(position, rope_width):
    half_width = rope_width // 2
    freq_steps = jnp.arange(half_width).astype(jnp.float32) * (2.0 / rope_width)
    frequency = jnp.exp(-math.log(ROPE_BASE) * freq_steps)
    return position.astype(jnp.float32)[:, None] * frequency[None, :]


def rotate(values, rot_angle):
    half_width = values.shape[-1] // 2
    first_half = values[..., :half_width].astype(jnp.float32)
    second_half = values[..., half_width:].astype(jnp.float32)
    cosine = jnp.cos(rot_angle)
    sine_part = jnp.sin(rot_angle)
    return jnp.concatenate(
        [
            first_half * cosine - second_half * sine_part,
            first_half * sine_part + second_half * cosine,
        ],
        axis=-1,
    )


def request_of(req_len, token_index):
    req_ends = jnp.cumsum(req_len)
    return jnp.sum((token_index[:, None] >= req_ends[None, :]).astype(jnp.int32), axis=1)


def position_of(req_len, req_offset, token_index):
    request = request_of(req_len, token_index)
    req_ends = jnp.cumsum(req_len)
    starts = req_ends - req_len
    member = request[:, None] == jnp.arange(req_len.shape[0])[None, :]
    start_at = jnp.sum(jnp.where(member, starts[None, :], 0), axis=1)
    offset = jnp.sum(jnp.where(member, req_offset[None, :], 0), axis=1)
    return offset + token_index - start_at


def key_width(piece_rows):
    for option_width in (1024, 512, 256, 128):
        return option_width
    return piece_rows


def body(
    hidden,
    queries,
    req_len,
    req_offset,
    expert_ids,
    decode_slot,
    attn_gain,
    kv_down,
    kv_gain,
    key_up,
    value_up,
    out_proj,
    ffn_gain,
    router,
    expert_gate_up,
    expert_down,
):
    head_count = lax.axis_size("head")
    seq_place = lax.axis_index("seq")
    head_place = lax.axis_index("head")
    tok_rows = hidden.shape[0]
    heads_here = key_up.shape[0]
    my_index = seq_place * tok_rows + jnp.arange(tok_rows, dtype=jnp.int32)
    my_request = request_of(req_len, my_index)
    my_turn = angles(position_of(req_len, req_offset, my_index), ROPE)
    normed = rms_rows(hidden, attn_gain).astype(jnp.bfloat16)
    head_view = queries.reshape(tok_rows, heads_here, NOPE + ROPE)
    query_rope = rotate(head_view[:, :, NOPE:], my_turn[:, None, :]).astype(jnp.bfloat16)
    query_latent = jnp.einsum(
        "thn,hnc->thc", head_view[:, :, :NOPE], key_up, preferred_element_type=jnp.float32
    ).astype(jnp.bfloat16)
    query_rows = tok_rows * heads_here
    flat_latent = query_latent.reshape(query_rows, KV_RANK)
    flat_rope = query_rope.reshape(query_rows, ROPE)
    row_token = jnp.repeat(my_index, heads_here)
    row_request = jnp.repeat(my_request, heads_here)
    score_scale = 1.0 / math.sqrt(NOPE + ROPE)
    my_device = seq_place * head_count + head_place
    slot_ids = my_device * DEC_SLOTS + jnp.arange(DEC_SLOTS, dtype=jnp.int32)
    block_ids = jnp.arange(decode_slot.shape[0], dtype=jnp.int32)
    slot_match = decode_slot[None, :] == slot_ids[:, None]
    source_block = jnp.sum(jnp.where(slot_match, block_ids[None, :], 0), axis=1)
    slot_filled = jnp.any(slot_match, axis=1)
    kv_full = jnp.dot(normed, kv_down, preferred_element_type=jnp.float32)
    latent = rms_rows(kv_full[:, :KV_RANK], kv_gain).astype(jnp.bfloat16)
    key_rope = rotate(kv_full[:, KV_RANK:], my_turn).astype(jnp.bfloat16)
    run_peak = jnp.full((query_rows,), MASKED, jnp.float32)
    run_total = jnp.zeros((query_rows,), jnp.float32)
    run_acc = jnp.zeros((query_rows, KV_RANK), jnp.float32)
    piece_latent = lax.all_gather(latent, "seq", axis=0, tiled=True)
    piece_rope = lax.all_gather(key_rope, "seq", axis=0, tiled=True)
    piece_rows = piece_latent.shape[0]
    block_width = key_width(piece_rows)

    def key_block(block_no, loop_state):
        peak_now, total_now, acc_now = loop_state
        offset_rows = block_no * block_width
        block_latent = lax.dynamic_slice_in_dim(piece_latent, offset_rows, block_width, 0)
        block_rope = lax.dynamic_slice_in_dim(piece_rope, offset_rows, block_width, 0)
        key_index = offset_rows + jnp.arange(block_width, dtype=jnp.int32)
        key_request = request_of(req_len, key_index)
        contract = (((1,), (1,)), ((), ()))
        scores = lax.dot_general(
            flat_latent, block_latent, contract, preferred_element_type=jnp.float32
        )
        scores = (
            scores
            + lax.dot_general(flat_rope, block_rope, contract, preferred_element_type=jnp.float32)
        ) * score_scale
        allowed = (key_index[None, :] <= row_token[:, None]) & (
            key_request[None, :] == row_request[:, None]
        )
        scores = jnp.where(allowed, scores, MASKED)
        new_peak = jnp.maximum(peak_now, jnp.max(scores, axis=1))
        exp_terms = jnp.where(allowed, jnp.exp(scores - new_peak[:, None]), 0.0)
        fade_factor = jnp.exp(peak_now - new_peak)
        total_now = total_now * fade_factor + jnp.sum(exp_terms, axis=1)
        acc_now = acc_now * fade_factor[:, None] + jnp.dot(
            exp_terms.astype(jnp.bfloat16), block_latent, preferred_element_type=jnp.float32
        )
        return (new_peak, total_now, acc_now)

    run_peak, run_total, run_acc = lax.fori_loop(
        0, piece_rows // block_width, key_block, (run_peak, run_total, run_acc)
    )
    block_count = piece_rows // BLOCK
    pick_matrix = (
        source_block[:, None] == jnp.arange(block_count, dtype=jnp.int32)[None, :]
    ) & slot_filled[:, None]
    pick_matrix = pick_matrix.astype(jnp.bfloat16)
    slot_latent = jnp.dot(
        pick_matrix,
        piece_latent.reshape(block_count, BLOCK * KV_RANK),
        preferred_element_type=jnp.float32,
    )
    slot_rope = jnp.dot(
        pick_matrix,
        piece_rope.reshape(block_count, BLOCK * ROPE),
        preferred_element_type=jnp.float32,
    )
    folded = (run_peak, run_total, run_acc, slot_latent, slot_rope)
    run_total = folded[1]
    run_acc = folded[2]
    slot_latent = folded[3]
    slot_rope = folded[4]
    attended = (
        (run_acc / run_total[:, None]).astype(jnp.bfloat16).reshape(tok_rows, heads_here, KV_RANK)
    )
    head_out = jnp.einsum(
        "thc,hcv->thv", attended, value_up, preferred_element_type=jnp.float32
    ).astype(jnp.bfloat16)
    attn_part = jnp.dot(
        head_out.reshape(tok_rows, heads_here * V_HEAD),
        out_proj,
        preferred_element_type=jnp.float32,
    )
    mixed_rows = hidden.astype(jnp.float32) + lax.psum(
        attn_part.astype(jnp.bfloat16), "head"
    ).astype(jnp.float32)
    moe_in = rms_rows(mixed_rows, ffn_gain).astype(jnp.bfloat16)
    expert_count = router.shape[1]
    capacity = max(2, tok_rows * TOP * 4 // (3 * expert_count))
    gate_score = jax.nn.sigmoid(
        jnp.dot(moe_in.astype(jnp.float32), router, precision=lax.Precision.HIGHEST)
    )
    expert_axis = jnp.arange(expert_count, dtype=jnp.int32)
    id_match = expert_ids[:, :, None] == expert_axis[None, None, :]
    chosen = jnp.sum(jnp.where(id_match, gate_score[:, None, :], 0.0), axis=2)
    gate_weight = ROUTE_SCALE * chosen / jnp.sum(chosen, axis=1, keepdims=True)
    flat_ids = expert_ids.reshape(-1)
    one_hot = (flat_ids[:, None] == expert_axis[None, :]).astype(jnp.int32)
    earlier = jnp.cumsum(one_hot, axis=0) - one_hot
    slot_rank = jnp.sum(earlier * one_hot, axis=1)
    flat_slot = flat_ids * capacity + slot_rank
    owner_token = jnp.repeat(jnp.arange(tok_rows, dtype=jnp.int32), TOP)
    slot_token = jnp.zeros((expert_count * capacity,), jnp.int32).at[flat_slot].set(owner_token)
    slot_used = jnp.zeros((expert_count * capacity,), jnp.bool_).at[flat_slot].set(True)
    send_rows = jnp.where(
        slot_used[:, None], moe_in[slot_token], jnp.zeros((), jnp.bfloat16)
    ).reshape(expert_count, capacity, D)
    gate_up_local = expert_gate_up[0]
    down_local = expert_down[0]
    quarter_cols = D // head_count
    arrived = lax.all_to_all(send_rows, "seq", split_axis=0, concat_axis=0, tiled=True)
    sources, item_count, width_cols = arrived.shape
    flat_rows = arrived.reshape(sources * item_count, width_cols)
    gate_part = jnp.dot(flat_rows, gate_up_local[0], preferred_element_type=jnp.float32)
    up_part = jnp.dot(flat_rows, gate_up_local[1], preferred_element_type=jnp.float32)
    activated = (jax.nn.silu(gate_part) * up_part).astype(jnp.bfloat16)
    part_out = (
        jnp.dot(activated, down_local, preferred_element_type=jnp.float32)
        .astype(jnp.bfloat16)
        .reshape(sources, item_count, width_cols)
    )
    returned = lax.all_to_all(part_out, "seq", split_axis=0, concat_axis=0, tiled=True)
    back_cols = returned.shape[2]
    picked = returned.reshape(expert_count * capacity, back_cols)[flat_slot].reshape(
        tok_rows, TOP, back_cols
    )
    weighted = jnp.sum(picked.astype(jnp.float32) * gate_weight[:, :, None], axis=1)
    moe_out = lax.psum_scatter(
        weighted.astype(jnp.bfloat16), "head", scatter_dimension=1, tiled=True
    ).astype(jnp.float32)
    residual_part = lax.dynamic_slice_in_dim(mixed_rows, head_place * quarter_cols, quarter_cols, 1)
    output = (residual_part + moe_out).astype(jnp.bfloat16)
    decode_latent = slot_latent.astype(jnp.bfloat16).reshape(DEC_SLOTS, BLOCK, KV_RANK)
    decode_rope = slot_rope.astype(jnp.bfloat16)
    return (output, decode_latent, decode_rope)


def solution(mesh):
    placed = (
        P("seq", None),
        P("seq", "head"),
        P(),
        P(),
        P("seq", None),
        P(),
        P(),
        P(),
        P(),
        P("head", None, None),
        P("head", None, None),
        P("head", None),
        P(),
        P(),
        P("seq", None, None, "head"),
        P("seq", "head", None),
    )
    return jax.shard_map(
        body,
        mesh=mesh,
        in_specs=placed,
        out_specs=(P("seq", "head"), P(("seq", "head"), None, None), P(("seq", "head"), None)),
        check_vma=False,
    )
```

profile of v0, /device:TPU:14, one launch (start us, length us, event | category | flops | bytes accessed | tf_op | source)
XLA Modules:
  0.0 398.2 jit_solution(13828456274183690813)
XLA Ops:
  8.6 2.7 fusion.47
  19.5 32.4 %all_gather.7 = bf16[2048,64]{0,1:T(8,128)(2,1)} all-gather(bf16[128,64]{0,1:T(8,128)(2,1)S(1)} %pad_maximum_fusion.1), channel_id=1, replica_groups=mesh['seq'=16,'head'=2] {'seq'}, dimensions={0}, use_global_device_ids=true | all-gather | bytes 278528 | tf_op jit(solution)/shard_map/all_gather | solution.py:121
  63.5 12.5 %all-gather.2.cloned.1.call-done = bf16[2048,512]{0,1:T(8,128)(2,1)} async-done(((bf16[128,512]{0,1:T(8,128)(2,1)}), bf16[2048,512]{0,1:T(8,128)(2,1)}) %all-gather.2.cloned.1.call-update) | async-done | bytes 2097168 | tf_op jit(solution)/shard_map/all_gather | solution.py:120
  76.1 4.0 copy.49
  80.0 20.3 %while.20 = (s32[]{:T(128)}, f32[1024]{0:T(1024)S(1)}, f32[1024]{0:T(1024)S(1)}, f32[1024,512]{1,0:T(8,128)}, s32[1,2]{1,0:T(1,128)}, /*index=5*/bf16[2048,512]{...) while((s32[]{:T(128)}, f32[1024]{0:T(1024)S(1)}, ...), condition=%wide.region_11.12_spmd.clone, body=%wide.region_7.11_spmd.clone.sunk | while | flops 2303208448 | bytes 58217812 | solution.py:153
  100.3 2.0 fusion.44
  102.4 2.2 convolution_convert_fusion.4
  106.6 3.6 scatter_custom_fusion
  110.4 3.4 scatter_custom_fusion.1
  113.8 12.2 %all-reduce.2.cloned.1.call-done = bf16[128,2048]{1,0:T(8,128)(2,1)} async-done(((bf16[128,2048]{1,0:T(8,128)(2,1)}), bf16[128,2048]{1,0:T(8,128)(2,1)}) %all-reduce.2.cloned.1.call-update) | async-done | bytes 524304 | tf_op jit(solution)/shard_map/psum | solution.py:187
  126.1 2.3 convert_add_fusion
  129.8 6.0 %gather_fusion = bf16[1024,2048]{1,0:T(8,128)(2,1)} fusion(bf16[128,2048]{1,0:T(8,128)(2,1)S(1)} %multiply_convert_fusion.1, s32[1024]{0:T(1024)S(1)} %fusion.60), kind=kCustom, calls=%fused_computation | custom fusion | bytes 8392704 | tf_op jit(solution)/shard_map/gather | solution.py:209
  135.9 2.5 broadcast_select_fusion
  138.4 98.9 %all_to_all.10 = bf16[16,64,2048]{2,1,0:T(8,128)(2,1)S(1)} all-to-all(bf16[16,64,2048]{2,1,0:T(8,128)(2,1)S(1)} %broadcast_select_fusion), channel_id=1, replica_groups=mesh['seq'=16,'head'=2] {'seq'}, dimensions={0} | all-to-all | bytes 8388608 | tf_op jit(solution)/shard_map/all_to_all | solution.py:214
  237.3 2.0 copy-done.5
  239.3 6.6 %fusion.28 = f32[1024,704]{0,1:T(8,128)} fusion(bf16[1024,2048]{1,0:T(8,128)(2,1)S(1)} %bitcast.84, bf16[1,2,2048,704]{2,3,1,0:T(8,128)(2,1)} %param.32), kind=kOutput, calls=%fused_computation.40 | convolution fusion | flops 2952790016 | bytes 9961472 | tf_op jit(solution)/shard_map/dot_general | solution.py:218
  245.9 11.3 %convolution_convert_fusion.1 = bf16[1024,2048]{1,0:T(8,128)(2,1)} fusion(bf16[1,704,2048]{2,1,0:T(8,128)(2,1)S(1)} %copy-done, f32[1024,704]{0,1:T(8,128)} %fusion.28, bf16[1024,2048]{1,0:T(8,128)(2,1)} %bitcast.85, bf16[1,2,2048,704]{2,3,1,0:T(8,128)(2,1)} %param.32), kind=kOutput, calls=%fused_computation.38 | convolution fusion | flops 5912002560 | bytes 17039360 | tf_op jit(solution)/shard_map/dot_general | solution.py:221
  257.2 6.5 %all-to-all-start.1 = ((bf16[16,64,2048]{2,1,0:T(8,128)(2,1)}), bf16[16,64,2048]{2,1,0:T(8,128)(2,1)}, u32[]{:S(2)}, u32[]{:S(2)}) async-start(bf16[16,64,2048]{2,1,0:T(8,128)(2,1)} %bitcast.83), calls=%async_computation.1 | async-start | bytes 8388608 | tf_op jit(solution)/shard_map/all_to_all | solution.py:225
  264.7 91.1 %all-to-all-done.1 = bf16[16,64,2048]{2,1,0:T(8,128)(2,1)} async-done(((bf16[16,64,2048]{2,1,0:T(8,128)(2,1)}), bf16[16,64,2048]{2,1,0:T(8,128)(2,1)}, u32[]{:S(2)}, u32[]{:S(2)}) %all-to-all-start.1) | async-done | bytes 4194336 | tf_op jit(solution)/shard_map/all_to_all | solution.py:225
  355.8 9.8 %gather_fusion.1 = bf16[768,2048]{1,0:T(8,128)(2,1)} fusion(bf16[1024,2048]{1,0:T(8,128)(2,1)} %bitcast.18, s32[1024]{0:T(1024)S(1)} %pad_clamp_fusion), kind=kCustom, calls=%fused_computation.1 | custom fusion | bytes 6294528 | tf_op jit(solution)/shard_map/gather | solution.py:227
  365.7 6.6 %reshape.294 = f32[128,6,2048]{2,1,0:T(8,128)} reshape(bf16[768,2048]{1,0:T(8,128)(2,1)} %gather_fusion.1) | data formatting | bytes 9437184 | tf_op jit(solution)/shard_map/convert_element_type | solution.py:230
  372.2 7.5 %multiply_reduce_fusion = bf16[128,2048]{1,0:T(8,128)(2,1)} fusion(f32[128,6,2048]{2,1,0:T(8,128)} %reshape.294, f32[128,6]{1,0:T(8,128)S(1)} %copy.57), kind=kLoop, calls=%fused_computation.36 | loop fusion | flops 2883584 | bytes 6818816 | tf_op jit(solution)/shard_map/reduce_sum | solution.py:230
  382.9 4.2 %reshape.291 = bf16[128,8192]{1,0:T(8,128)(2,1)} reshape(bf16[2048,512]{1,0:T(8,128)(2,1)} %get-tuple-element.499) | data formatting | bytes 4194304 | tf_op jit(solution)/shard_map/reshape | solution.py:163
  387.1 2.0 convolution_convert_fusion
  (136 shorter events, 51.5 us)
Async XLA Ops:
  7.2 238.7 %copy-start = (bf16[1,704,2048]{2,1,0:T(8,128)(2,1)S(1)}, bf16[1,704,2048]{2,1,0:T(8,128)(2,1)}, u32[]{:S(2)}) copy-start(bf16[1,704,2048]{2,1,0:T(8,128)(2,1)} %param.33) | copy-start | bytes 8650756
  7.2 5.9 %copy-start.12 = (s32[128,6]{0,1:T(8,128)S(1)}, s32[128,6]{0,1:T(8,128)}, u32[]{:S(2)}) copy-start(s32[128,6]{0,1:T(8,128)} %param.22) | copy-start | bytes 9220
  7.2 6.8 %copy-start.17 = (s32[2]{0:T(128)S(1)}, s32[2]{0:T(128)}, u32[]{:S(2)}) copy-start(s32[2]{0:T(128)} %param.20) | copy-start | bytes 28
  7.2 11.4 %copy-start.16 = (s32[2]{0:T(128)S(1)}, s32[2]{0:T(128)}, u32[]{:S(2)}) copy-start(s32[2]{0:T(128)} %param.21) | copy-start | bytes 28
  7.2 68.8 %all-gather.2.cloned.1.call-start = ((), (), s32[]{:S(2)}) async-start(), calls=%async_computation.3 | async-start | bytes 2228224 | tf_op jit(solution)/shard_map/all_gather | solution.py:120
  13.0 113.1 %all-reduce.2.cloned.1.call-start = ((), (), s32[]{:S(2)}) async-start(), calls=%async_computation.4 | async-start | bytes 1048576 | tf_op jit(solution)/shard_map/psum | solution.py:187
  59.2 3.4 copy-start.8
  59.3 3.4 copy-start.9
  81.7 1.8 copy-start.3
  81.7 1.9 copy-start.10
  85.3 1.6 copy-start.6
  91.8 1.8 copy-start.3
  91.8 1.9 copy-start.10
  100.3 5.8 %copy-start.1 = (bf16[2048,64]{1,0:T(8,128)(2,1)}, bf16[2048,64]{1,0:T(8,128)(2,1)S(1)}, u32[]{:S(2)}) copy-start(bf16[2048,64]{1,0:T(8,128)(2,1)S(1)} %get-tuple-element.498) | copy-start | bytes 786436
  100.3 4.3 %copy-start.4 = (bf16[1024,2048]{1,0:T(8,128)(2,1)S(1)}, bf16[1024,2048]{1,0:T(8,128)(2,1)}, u32[]{:S(2)}) copy-start(bf16[1024,2048]{1,0:T(8,128)(2,1)} %param.29) | copy-start | bytes 12582916
  102.4 4.1 %copy-start.13 = (s32[768]{0:T(1024)S(1)}, s32[768]{0:T(1024)}, u32[]{:S(2)}) copy-start(s32[768]{0:T(1024)} %eq.123) | copy-start | bytes 9220
  102.4 4.2 %copy-start.14 = (s32[768,1]{0,1:T(1,128)S(1)}, s32[768,1]{0,1:T(1,128)}, u32[]{:S(2)}) copy-start(s32[768,1]{0,1:T(1,128)} %mul.268) | copy-start | bytes 9220
  104.6 23.8 %copy-start.15 = (f32[2048]{0:T(1024)S(1)}, f32[2048]{0:T(1024)}, u32[]{:S(2)}) copy-start(f32[2048]{0:T(1024)} %param.30) | copy-start | bytes 24580
  237.3 2.0 copy-start.5
  257.2 6.8 %copy-start.11 = (f32[2048,16]{0,1:T(8,128)S(1)}, f32[2048,16]{0,1:T(8,128)}, u32[]{:S(2)}) copy-start(f32[2048,16]{0,1:T(8,128)} %param.31) | copy-start | bytes 393220
  257.2 98.7 %all-to-all-start.1 = ((bf16[16,64,2048]{2,1,0:T(8,128)(2,1)}), bf16[16,64,2048]{2,1,0:T(8,128)(2,1)}, u32[]{:S(2)}, u32[]{:S(2)}) async-start(bf16[16,64,2048]{2,1,0:T(8,128)(2,1)} %bitcast.83), calls=%async_computation.1 | async-start | bytes 8388608 | tf_op jit(solution)/shard_map/all_to_all | solution.py:225
  263.7 126.1 %reduce-scatter.2.cloned.1.call-start = ((), (), s32[]{:S(2)}) async-start(), calls=%async_computation.5 | async-start | bytes 786432 | tf_op jit(solution)/shard_map/reduce_scatter | solution.py:231
  372.2 7.5 %copy-start.2 = (bf16[2048,64]{1,0:T(8,128)(2,1)S(1)}, bf16[2048,64]{1,0:T(8,128)(2,1)}, u32[]{:S(2)}) copy-start(bf16[2048,64]{1,0:T(8,128)(2,1)} %copy-done.1) | copy-start | bytes 786436
  372.2 8.6 %copy-start.18 = (s32[128]{0:T(128)S(1)}, s32[128]{0:T(128)}, u32[]{:S(2)}) copy-start(s32[128]{0:T(128)} %param.23) | copy-start | bytes 1540
  (3 other events, 4.3 us)
Sparse Core Ops, SparseCore 0:
  13.1 62.9 all-gather.1
  106.3 19.6 all-reduce.1
  379.8 7.2 reduce-scatter.1
where the time goes:
time: 399 us; the launch traced here: 398 us
  blocking collectives  131 us (33%)
  waiting for transfers between devices  116 us (29%)
  local copies, waits for them, and re-layouts  56 us (14%)
  matrix products  41.4 us (10%)
  other arithmetic  32.5 us (8%)
  between operations  14 us (4%)
  starting transfers between devices  6.86 us (2%)
    all_to_all x1, blocking collectives, body(): lax.all_to_all(send_rows, 'seq', split_axis=0, concat_axis=0, tiled=True)  98.9 us
    all_to_all x1, waiting for transfers between devices, body(): lax.all_to_all(part_out, 'seq', split_axis=0, concat_axis=0, tiled=True)  91.1 us
    all_gather x1, blocking collectives, body(): piece_rope = lax.all_gather(key_rope, 'seq', axis=0, tiled=True)  32.4 us
    all_gather x1, waiting for transfers between devices, body(): piece_latent = lax.all_gather(latent, 'seq', axis=0, tiled=True)  12.5 us
    psum x1, waiting for transfers between devices, body(): lax.psum(attn_part.astype(jnp.bfloat16), 'head').astype(jnp.float32)  12.2 us
    dot_general x1, matrix products, body(): jnp.dot(activated, down_local, preferred_element_type=jnp.float32)  11.3 us
    unnamed x35, local copies, waits for them, and re-layouts  9.92 us
    gather x1, local copies, waits for them, and re-layouts, body(): returned.reshape(expert_count * capacity, back_cols)[flat_slot]  9.82 us
  transfers between devices with their start and end apart: 4, of which 3 were waited for; matrix products, arithmetic and copies ran while one was open for 9% of the time, Pallas kernels for 0%

commit v1 on v0

--- a/solution.py
+++ b/solution.py
@@ -118,7 +118,12 @@
     run_total = jnp.zeros((query_rows,), jnp.float32)
     run_acc = jnp.zeros((query_rows, KV_RANK), jnp.float32)
     piece_latent = lax.all_gather(latent, "seq", axis=0, tiled=True)
-    piece_rope = lax.all_gather(key_rope, "seq", axis=0, tiled=True)
+    ring = [key_rope]
+    for hop in range(15):
+        ring.append(lax.ppermute(ring[-1], "seq", [(dev, (dev + 1) % 16) for dev in range(16)]))
+    piece_rope = jnp.roll(
+        jnp.concatenate(ring[::-1], axis=0), (lax.axis_index("seq") + 1) * ring[0].shape[0], axis=0
+    )
     piece_rows = piece_latent.shape[0]
     block_width = key_width(piece_rows)
 

time: 399 us -> 487 us (1.22)
  starting transfers between devices: 6.86 us -> 62.5 us
  blocking collectives: 131 us -> 98.9 us
  local copies, waits for them, and re-layouts: 56 us -> 84 us
  waiting for transfers between devices: 116 us -> 144 us
  other arithmetic: 32.5 us -> 37.5 us
    ppermute x0 -> x15, starting transfers between devices: none -> 55.6 us  [body(): lax.ppermute(ring[-1], 'seq', [(dev, (dev + 1) % 16) for dev in range(16)])]
    all_gather x1 -> x0, blocking collectives: 32.4 us -> none  [body(): piece_rope = lax.all_gather(key_rope, 'seq', axis=0, tiled=True)]
    unnamed x35 -> x85, local copies, waits for them, and re-layouts: 9.92 us -> 36.4 us
    ppermute x0 -> x15, waiting for transfers between devices: none -> 16.3 us  [body(): lax.ppermute(ring[-1], 'seq', [(dev, (dev + 1) % 16) for dev in range(16)])]
    psum x1, waiting for transfers between devices: 12.2 us -> 21.7 us  [body(): lax.psum(attn_part.astype(jnp.bfloat16), 'head').astype(jnp.float32)]
  transfers between devices with their start and end apart: 4 -> 19, of which waited for: 3 -> 15; matrix products, arithmetic and copies ran while one was open for 9% -> 13% of each run, Pallas kernels for 0% -> 0%
where the time goes in v1:
time: 487 us; the launch traced here: 484 us
  waiting for transfers between devices  144 us (30%)
  blocking collectives  98.9 us (20%)
  local copies, waits for them, and re-layouts  84 us (17%)
  starting transfers between devices  62.5 us (13%)
  matrix products  42.3 us (9%)
  other arithmetic  37.5 us (8%)
  between operations  14.1 us (3%)
    all_to_all x1, blocking collectives, body(): lax.all_to_all(send_rows, 'seq', split_axis=0, concat_axis=0, tiled=True)  98.9 us
    all_to_all x1, waiting for transfers between devices, body(): lax.all_to_all(part_out, 'seq', split_axis=0, concat_axis=0, tiled=True)  91.1 us
    ppermute x15, starting transfers between devices, body(): lax.ppermute(ring[-1], 'seq', [(dev, (dev + 1) % 16) for dev in range(16)])  55.6 us
    unnamed x85, local copies, waits for them, and re-layouts  36.4 us
    psum x1, waiting for transfers between devices, body(): lax.psum(attn_part.astype(jnp.bfloat16), 'head').astype(jnp.float32)  21.7 us
    ppermute x15, waiting for transfers between devices, body(): lax.ppermute(ring[-1], 'seq', [(dev, (dev + 1) % 16) for dev in range(16)])  16.3 us
    all_gather x1, waiting for transfers between devices, body(): piece_latent = lax.all_gather(latent, 'seq', axis=0, tiled=True)  15 us
    dot_general x1, matrix products, body(): jnp.dot(activated, down_local, preferred_element_type=jnp.float32)  11.3 us
  transfers between devices with their start and end apart: 19, of which 15 were waited for; matrix products, arithmetic and copies ran while one was open for 13% of the time, Pallas kernels for 0%

profile of v1, /device:TPU:14, one launch (start us, length us, event | category | flops | bytes accessed | tf_op | source)
XLA Modules:
  0.0 483.7 jit_solution(4462716957646552240)
XLA Ops:
  25.6 4.1 collective-permute-start.2
  31.8 4.1 collective-permute-start.3
  37.9 4.1 collective-permute-start.4
  44.0 4.1 collective-permute-start.5
  50.2 4.1 collective-permute-start.6
  56.3 4.1 collective-permute-start.7
  62.5 4.1 collective-permute-start.8
  68.0 4.1 collective-permute-start.9
  84.6 4.1 collective-permute-start.12
  90.2 4.2 collective-permute-start.13
  96.1 4.2 collective-permute-start.14
  135.9 15.0 %all-gather.2.cloned.1.call-done = bf16[2048,512]{0,1:T(8,128)(2,1)} async-done(((bf16[128,512]{0,1:T(8,128)(2,1)}), bf16[2048,512]{0,1:T(8,128)(2,1)}) %all-gather.2.cloned.1.call-update) | async-done | bytes 2097168 | tf_op jit(solution)/shard_map/all_gather | solution.py:120
  154.8 21.4 %while.20 = (s32[]{:T(128)}, f32[1024]{0:T(1024)S(1)}, f32[1024]{0:T(1024)S(1)}, f32[1024,512]{1,0:T(8,128)}, s32[1,2]{1,0:T(1,128)}, /*index=5*/bf16[2048,512]{...) while((s32[]{:T(128)}, f32[1024]{0:T(1024)S(1)}, ...), condition=%wide.region_11.12_spmd.clone, body=%wide.region_7.11_spmd.clone.sunk | while | flops 2303208448 | bytes 58217812 | solution.py:158
  189.8 21.7 %all-reduce.2.cloned.1.call-done = bf16[128,2048]{1,0:T(8,128)(2,1)} async-done(((bf16[128,2048]{1,0:T(8,128)(2,1)}), bf16[128,2048]{1,0:T(8,128)(2,1)}) %all-reduce.2.cloned.1.call-update) | async-done | bytes 524304 | tf_op jit(solution)/shard_map/psum | solution.py:192
  215.3 6.0 %gather_fusion = bf16[1024,2048]{1,0:T(8,128)(2,1)} fusion(bf16[128,2048]{1,0:T(8,128)(2,1)S(1)} %multiply_convert_fusion.1, s32[1024]{0:T(1024)S(1)} %fusion.60), kind=kCustom, calls=%fused_computation | custom fusion | bytes 8392704 | tf_op jit(solution)/shard_map/gather | solution.py:214
  223.8 98.9 %all_to_all.10 = bf16[16,64,2048]{2,1,0:T(8,128)(2,1)S(1)} all-to-all(bf16[16,64,2048]{2,1,0:T(8,128)(2,1)S(1)} %broadcast_select_fusion), channel_id=1, replica_groups=mesh['seq'=16,'head'=2] {'seq'}, dimensions={0} | all-to-all | bytes 8388608 | tf_op jit(solution)/shard_map/all_to_all | solution.py:219
  324.7 6.6 %fusion.28 = f32[1024,704]{0,1:T(8,128)} fusion(bf16[1024,2048]{1,0:T(8,128)(2,1)S(1)} %bitcast.84, bf16[1,2,2048,704]{2,3,1,0:T(8,128)(2,1)} %param.32), kind=kOutput, calls=%fused_computation.40 | convolution fusion | flops 2952790016 | bytes 9961472 | tf_op jit(solution)/shard_map/dot_general | solution.py:223
  331.3 11.3 %convolution_convert_fusion.1 = bf16[1024,2048]{1,0:T(8,128)(2,1)} fusion(bf16[1,704,2048]{2,1,0:T(8,128)(2,1)S(1)} %copy-done, f32[1024,704]{0,1:T(8,128)} %fusion.28, bf16[1024,2048]{1,0:T(8,128)(2,1)} %bitcast.85, bf16[1,2,2048,704]{2,3,1,0:T(8,128)(2,1)} %param.32), kind=kOutput, calls=%fused_computation.38 | convolution fusion | flops 5912002560 | bytes 17039360 | tf_op jit(solution)/shard_map/dot_general | solution.py:226
  342.6 6.5 %all-to-all-start.1 = ((bf16[16,64,2048]{2,1,0:T(8,128)(2,1)}), bf16[16,64,2048]{2,1,0:T(8,128)(2,1)}, u32[]{:S(2)}, u32[]{:S(2)}) async-start(bf16[16,64,2048]{2,1,0:T(8,128)(2,1)} %bitcast.83), calls=%async_computation.1 | async-start | bytes 8388608 | tf_op jit(solution)/shard_map/all_to_all | solution.py:230
  350.1 91.1 %all-to-all-done.1 = bf16[16,64,2048]{2,1,0:T(8,128)(2,1)} async-done(((bf16[16,64,2048]{2,1,0:T(8,128)(2,1)}), bf16[16,64,2048]{2,1,0:T(8,128)(2,1)}, u32[]{:S(2)}, u32[]{:S(2)}) %all-to-all-start.1) | async-done | bytes 4194336 | tf_op jit(solution)/shard_map/all_to_all | solution.py:230
  441.2 9.8 %gather_fusion.1 = bf16[768,2048]{1,0:T(8,128)(2,1)} fusion(bf16[1024,2048]{1,0:T(8,128)(2,1)} %bitcast.18, s32[1024]{0:T(1024)S(1)} %pad_clamp_fusion), kind=kCustom, calls=%fused_computation.1 | custom fusion | bytes 6294528 | tf_op jit(solution)/shard_map/gather | solution.py:232
  451.1 6.6 %reshape.294 = f32[128,6,2048]{2,1,0:T(8,128)} reshape(bf16[768,2048]{1,0:T(8,128)(2,1)} %gather_fusion.1) | data formatting | bytes 9437184 | tf_op jit(solution)/shard_map/convert_element_type | solution.py:235
  457.6 7.5 %multiply_reduce_fusion = bf16[128,2048]{1,0:T(8,128)(2,1)} fusion(f32[128,6,2048]{2,1,0:T(8,128)} %reshape.294, f32[128,6]{1,0:T(8,128)S(1)} %copy.57), kind=kLoop, calls=%fused_computation.36 | loop fusion | flops 2883584 | bytes 6818816 | tf_op jit(solution)/shard_map/reduce_sum | solution.py:235
  468.3 4.2 reshape.291
  (218 shorter events, 138.8 us)
Async XLA Ops:
  7.2 324.1 %copy-start = (bf16[1,704,2048]{2,1,0:T(8,128)(2,1)S(1)}, bf16[1,704,2048]{2,1,0:T(8,128)(2,1)}, u32[]{:S(2)}) copy-start(bf16[1,704,2048]{2,1,0:T(8,128)(2,1)} %param.33) | copy-start | bytes 8650756
  7.2 76.0 %copy-start.23 = (s32[128,6]{0,1:T(8,128)S(1)}, s32[128,6]{0,1:T(8,128)}, u32[]{:S(2)}) copy-start(s32[128,6]{0,1:T(8,128)} %param.22) | copy-start | bytes 9220
  7.2 143.7 %all-gather.2.cloned.1.call-start = ((), (), s32[]{:S(2)}) async-start(), calls=%async_computation.3 | async-start | bytes 2228224 | tf_op jit(solution)/shard_map/all_gather | solution.py:120
  16.0 3.7 collective-permute-start
  20.3 4.7 collective-permute-start.1
  25.6 5.5 %collective-permute-start.2 = (bf16[128,64]{0,1:T(8,128)(2,1)S(1)}, bf16[128,64]{0,1:T(8,128)(2,1)S(1)}, u32[]{:S(2)}, u32[]{:S(2)}) collective-permute-start(bf16[128,64]{0,1:T(8,128)(2,1)S(1)} %collective-permute-done.1), channel_id=1, source_target_pairs={{0,2},{2,4},{4,6},{6,8},{8,10},{10,12},{12,14},{14,16},{16,18},{18... | collective-permute-start | bytes 49160 | tf_op jit(solution)/shard_map/ppermute | solution.py:123
  31.8 5.5 %collective-permute-start.3 = (bf16[128,64]{0,1:T(8,128)(2,1)S(1)}, bf16[128,64]{0,1:T(8,128)(2,1)S(1)}, u32[]{:S(2)}, u32[]{:S(2)}) collective-permute-start(bf16[128,64]{0,1:T(8,128)(2,1)S(1)} %collective-permute-done.2), channel_id=1, source_target_pairs={{0,2},{2,4},{4,6},{6,8},{8,10},{10,12},{12,14},{14,16},{16,18},{18... | collective-permute-start | bytes 49160 | tf_op jit(solution)/shard_map/ppermute | solution.py:123
  37.9 5.5 %collective-permute-start.4 = (bf16[128,64]{0,1:T(8,128)(2,1)S(1)}, bf16[128,64]{0,1:T(8,128)(2,1)S(1)}, u32[]{:S(2)}, u32[]{:S(2)}) collective-permute-start(bf16[128,64]{0,1:T(8,128)(2,1)S(1)} %collective-permute-done.3), channel_id=1, source_target_pairs={{0,2},{2,4},{4,6},{6,8},{8,10},{10,12},{12,14},{14,16},{16,18},{18... | collective-permute-start | bytes 49160 | tf_op jit(solution)/shard_map/ppermute | solution.py:123
  44.0 5.5 %collective-permute-start.5 = (bf16[128,64]{0,1:T(8,128)(2,1)S(1)}, bf16[128,64]{0,1:T(8,128)(2,1)S(1)}, u32[]{:S(2)}, u32[]{:S(2)}) collective-permute-start(bf16[128,64]{0,1:T(8,128)(2,1)S(1)} %collective-permute-done.4), channel_id=1, source_target_pairs={{0,2},{2,4},{4,6},{6,8},{8,10},{10,12},{12,14},{14,16},{16,18},{18... | collective-permute-start | bytes 49160 | tf_op jit(solution)/shard_map/ppermute | solution.py:123
  50.2 5.5 %collective-permute-start.6 = (bf16[128,64]{0,1:T(8,128)(2,1)S(1)}, bf16[128,64]{0,1:T(8,128)(2,1)S(1)}, u32[]{:S(2)}, u32[]{:S(2)}) collective-permute-start(bf16[128,64]{0,1:T(8,128)(2,1)S(1)} %collective-permute-done.5), channel_id=1, source_target_pairs={{0,2},{2,4},{4,6},{6,8},{8,10},{10,12},{12,14},{14,16},{16,18},{18... | collective-permute-start | bytes 49160 | tf_op jit(solution)/shard_map/ppermute | solution.py:123
  56.3 5.5 %collective-permute-start.7 = (bf16[128,64]{0,1:T(8,128)(2,1)S(1)}, bf16[128,64]{0,1:T(8,128)(2,1)S(1)}, u32[]{:S(2)}, u32[]{:S(2)}) collective-permute-start(bf16[128,64]{0,1:T(8,128)(2,1)S(1)} %collective-permute-done.6), channel_id=1, source_target_pairs={{0,2},{2,4},{4,6},{6,8},{8,10},{10,12},{12,14},{14,16},{16,18},{18... | collective-permute-start | bytes 49160 | tf_op jit(solution)/shard_map/ppermute | solution.py:123
  62.5 5.5 %collective-permute-start.8 = (bf16[128,64]{0,1:T(8,128)(2,1)S(1)}, bf16[128,64]{0,1:T(8,128)(2,1)S(1)}, u32[]{:S(2)}, u32[]{:S(2)}) collective-permute-start(bf16[128,64]{0,1:T(8,128)(2,1)S(1)} %collective-permute-done.7), channel_id=1, source_target_pairs={{0,2},{2,4},{4,6},{6,8},{8,10},{10,12},{12,14},{14,16},{16,18},{18... | collective-permute-start | bytes 49160 | tf_op jit(solution)/shard_map/ppermute | solution.py:123
  68.0 15.2 %copy-start.19 = (bf16[128,64]{0,1:T(8,128)(2,1)}, bf16[128,64]{0,1:T(8,128)(2,1)S(1)}, u32[]{:S(2)}) copy-start(bf16[128,64]{0,1:T(8,128)(2,1)S(1)} %collective-permute-done.8) | copy-start | bytes 49156
  68.0 6.9 %collective-permute-start.9 = (bf16[128,64]{0,1:T(8,128)(2,1)S(1)}, bf16[128,64]{0,1:T(8,128)(2,1)S(1)}, u32[]{:S(2)}, u32[]{:S(2)}) collective-permute-start(bf16[128,64]{0,1:T(8,128)(2,1)S(1)} %collective-permute-done.8), channel_id=1, source_target_pairs={{0,2},{2,4},{4,6},{6,8},{8,10},{10,12},{12,14},{14,16},{16,18},{18... | collective-permute-start | bytes 49160 | tf_op jit(solution)/shard_map/ppermute | solution.py:123
  73.6 137.9 %all-reduce.2.cloned.1.call-start = ((), (), s32[]{:S(2)}) async-start(), calls=%async_computation.4 | async-start | bytes 1048576 | tf_op jit(solution)/shard_map/psum | solution.py:192
  74.9 5.5 %collective-permute-start.10 = (bf16[128,64]{0,1:T(8,128)(2,1)S(1)}, bf16[128,64]{0,1:T(8,128)(2,1)S(1)}, u32[]{:S(2)}, u32[]{:S(2)}) collective-permute-start(bf16[128,64]{0,1:T(8,128)(2,1)S(1)} %collective-permute-done.9), channel_id=1, source_target_pairs={{0,2},{2,4},{4,6},{6,8},{8,10},{10,12},{12,14},{14,16},{16,18},{18... | collective-permute-start | bytes 49160 | tf_op jit(solution)/shard_map/ppermute | solution.py:123
  80.4 14.8 %copy-start.21 = (bf16[128,64]{0,1:T(8,128)(2,1)}, bf16[128,64]{0,1:T(8,128)(2,1)S(1)}, u32[]{:S(2)}) copy-start(bf16[128,64]{0,1:T(8,128)(2,1)S(1)} %collective-permute-done.10) | copy-start | bytes 49156
  80.4 4.3 collective-permute-start.11
  84.6 5.6 %collective-permute-start.12 = (bf16[128,64]{0,1:T(8,128)(2,1)S(1)}, bf16[128,64]{0,1:T(8,128)(2,1)}, u32[]{:S(2)}, u32[]{:S(2)}) collective-permute-start(bf16[128,64]{0,1:T(8,128)(2,1)S(1)} %collective-permute-done.11), channel_id=1, source_target_pairs={{0,2},{2,4},{4,6},{6,8},{8,10},{10,12},{12,14},{14,16},{16,18},{18... | collective-permute-start | bytes 49160 | tf_op jit(solution)/shard_map/ppermute | solution.py:123
  90.2 5.9 %collective-permute-start.13 = (bf16[128,64]{0,1:T(8,128)(2,1)}, bf16[128,64]{0,1:T(8,128)(2,1)}, u32[]{:S(2)}, u32[]{:S(2)}) collective-permute-start(bf16[128,64]{0,1:T(8,128)(2,1)} %collective-permute-done.12), channel_id=1, source_target_pairs={{0,2},{2,4},{4,6},{6,8},{8,10},{10,12},{12,14},{14,16},{16,18},{18... | collective-permute-start | bytes 49160 | tf_op jit(solution)/shard_map/ppermute | solution.py:123
  96.1 14.6 %collective-permute-start.14 = (bf16[128,64]{0,1:T(8,128)(2,1)}, bf16[128,64]{0,1:T(8,128)(2,1)}, u32[]{:S(2)}, u32[]{:S(2)}) collective-permute-start(bf16[128,64]{0,1:T(8,128)(2,1)} %collective-permute-done.13), channel_id=1, source_target_pairs={{0,2},{2,4},{4,6},{6,8},{8,10},{10,12},{12,14},{14,16},{16,18},{18... | collective-permute-start | bytes 49160 | tf_op jit(solution)/shard_map/ppermute | solution.py:123
  180.5 33.3 %copy-start.27 = (f32[2048]{0:T(1024)S(1)}, f32[2048]{0:T(1024)}, u32[]{:S(2)}) copy-start(f32[2048]{0:T(1024)} %param.30) | copy-start | bytes 24580
  342.6 98.6 %all-to-all-start.1 = ((bf16[16,64,2048]{2,1,0:T(8,128)(2,1)}), bf16[16,64,2048]{2,1,0:T(8,128)(2,1)}, u32[]{:S(2)}, u32[]{:S(2)}) async-start(bf16[16,64,2048]{2,1,0:T(8,128)(2,1)} %bitcast.83), calls=%async_computation.1 | async-start | bytes 8388608 | tf_op jit(solution)/shard_map/all_to_all | solution.py:230
  349.1 126.1 %reduce-scatter.2.cloned.1.call-start = ((), (), s32[]{:S(2)}) async-start(), calls=%async_computation.5 | async-start | bytes 786432 | tf_op jit(solution)/shard_map/reduce_scatter | solution.py:236
  (28 other events, 87.7 us)
Sparse Core Ops, SparseCore 0:
  73.7 77.1 all-gather.1
  182.2 29.1 all-reduce.1
  465.3 7.2 reduce-scatter.1
